TPU v7x, 256 devices: a whole 4x4x8 slice. The times are simulated.
256 devices in a mesh: slab: 64 (over z, y, core), tile: 4 (over x).
Axes of the slice: x: 4, y: 4, z: 8, core: 2. Of those that a mesh axis runs over, the one named last changes fastest.
Arguments:
- snapshots: bfloat16 [8192, 128, 256], P(('slab', 'tile')), may hold values from -1210 to 1210
- routes: int32 [8192, 1], P(('slab', 'tile')), may hold values from 0 to 3; in each aligned block of 32 rows (0 to 31, 32 to 63, ...) at most 10 rows name the same one
- sketch_matrix: bfloat16 [256, 128], replicated, may hold values from -0.375 to 0.375
Outputs:
- basis_rows: bfloat16 [10240, 128, 128], P(('slab', 'tile'))
- triangle: float32 [128, 128], replicated
Inputs may be any that keep to these rules, and one draw needn't show every extreme that they name: `routes`: among the 32 blocks of one device no owner value appears more than 10 times; a block with value o goes to tile o of its own slab.
All inputs are finite; a program needn't handle non-finite values.
Results may differ from a plain program's by a relative error of at most 0.0065.
Values may be sent and summed in bfloat16 or wider, within the bound.
A program may use at most 64 MiB of HBM per device.

v0:
```python
import math
import jax
import jax.numpy as jnp
from jax import lax
from jax.sharding import PartitionSpec as P

SEND = 10


def slot_selector(routes, tiles, slots):
    destination = routes[:, 0]
    owners = jnp.arange(tiles, dtype=jnp.int32)
    owner_hit = (destination[None, :] == owners[:, None]).astype(jnp.int32)
    earlier = jnp.cumsum(owner_hit, axis=1) - owner_hit
    slot_ids = jnp.arange(slots, dtype=jnp.int32)
    chosen = owner_hit[:, None, :] * (earlier[:, None, :] == slot_ids[None, :, None]).astype(
        jnp.int32
    )
    return chosen.reshape(tiles * slots, routes.shape[0]).astype(jnp.bfloat16)


def place_blocks(selector, block_data):
    block_count, cell_rows, width = block_data.shape
    flattened = jnp.dot(
        selector,
        block_data.reshape(block_count, cell_rows * width),
        preferred_element_type=jnp.float32,
    )
    return flattened.astype(jnp.bfloat16).reshape(selector.shape[0], cell_rows, width)


def global_factor(partial_gram):
    gram_matrix = lax.psum(partial_gram, ("slab", "tile"))
    return jnp.linalg.cholesky(gram_matrix)


def local(snapshots, routes, sketch_matrix):
    n_tile = lax.axis_size("tile")
    n_slab = lax.axis_size("slab")
    block_count, cell_rows, snap_width = snapshots.shape
    sketch_width = sketch_matrix.shape[1]
    cell_root = math.sqrt(block_count * cell_rows * n_slab * n_tile)
    selector = slot_selector(routes, n_tile, SEND)
    outgoing = place_blocks(selector, snapshots).reshape(n_tile, SEND, cell_rows, snap_width)
    product = jnp.einsum(
        "tjrc,cd->tjrd",
        lax.all_to_all(outgoing, "tile", split_axis=0, concat_axis=0, tiled=True),
        sketch_matrix,
        preferred_element_type=jnp.float32,
    )
    sketch = product.astype(jnp.bfloat16)
    sketch_rows = sketch.reshape(-1, sketch_width)
    partial_gram = lax.dot_general(
        sketch_rows, sketch_rows, (((0,), (0,)), ((), ())), preferred_element_type=jnp.float32
    )
    lower_factor = global_factor(partial_gram)
    identity = jnp.eye(sketch_width, dtype=jnp.float32)
    inverse_factor = jax.scipy.linalg.solve_triangular(lower_factor, identity, lower=True)
    wide_rows = sketch_rows.astype(jnp.float32)
    scaled = (
        jnp.dot(wide_rows, inverse_factor.T, precision=lax.Precision.HIGHEST) * cell_root
    ).astype(jnp.bfloat16)
    basis_rows = scaled.reshape(n_tile * SEND, cell_rows, sketch_width)
    return (basis_rows, lower_factor.T / cell_root)


def solution(mesh):
    return jax.shard_map(
        local,
        mesh=mesh,
        in_specs=(P(("slab", "tile"), None, None), P(("slab", "tile"), None), P()),
        out_specs=(P(("slab", "tile"), None, None), P()),
        check_vma=False,
    )
```

profile of v0, /device:TPU:1, one launch (start us, length us, event | category | flops | bytes accessed | tf_op | source)
XLA Modules:
  0.0 325.9 jit_solution(3418719268438397038)
XLA Ops:
  7.2 0.0 copy-start
  7.2 0.0 all-reduce.2.cloned.1.call-start
  7.2 0.7 fusion.5
  7.9 0.2 reduce_window_sum.11
  8.1 0.7 fusion.6
  8.8 2.8 copy.17
  11.6 0.8 convolution_convert_fusion
  12.4 0.6 copy.18
  13.0 35.5 %all_to_all.5 = bf16[4,10,128,256]{3,2,1,0:T(8,128)(2,1)S(1)} all-to-all(bf16[4,10,128,256]{3,2,1,0:T(8,128)(2,1)S(1)} %bitcast.35), channel_id=1, replica_groups=mesh['slab'=64,'tile'=4] {'tile'}, dimensions={0} | all-to-all | bytes 5242880 | tf_op jit(solution)/shard_map/all_to_all | solution.py:47
  48.6 0.0 copy-done
  48.6 0.8 convolution_convert_fusion.1
  49.4 1.2 convolution_bitcast_fusion
  50.6 0.0 all-reduce.2.cloned.1.call-update
  50.6 240.6 %all-reduce.2.cloned.1.call-done = f32[128,128]{0,1:T(8,128)} async-done(((f32[128,128]{0,1:T(8,128)}), f32[128,128]{0,1:T(8,128)}) %all-reduce.2.cloned.1.call-update) | async-done | bytes 65552 | tf_op jit(solution)/shard_map/psum | solution.py:33
  291.2 0.9 copy.11
  292.1 0.9 fusion.4
  293.0 11.7 %cholesky.17 = f32[128,128]{1,0:T(8,128)S(1)} custom-call(f32[128,128]{1,0:T(8,128)S(1)} %fusion.4), custom_call_target="Cholesky" | custom-call | tf_op jit(solution)/shard_map/jit(cholesky)/cholesky | solution.py:34
  304.7 0.6 compare_reduce_fusion
  305.4 0.7 multiply_bitcast_fusion
  306.0 0.7 copy.12
  306.8 9.8 %custom-call.7 = f32[1,128,128]{1,2,0:T(8,128)S(1)} custom-call(f32[1,128,128]{2,1,0:T(8,128)S(1)} %get-tuple-element.7), custom_call_target="InvertDiagBlocksLowerTriangular" | custom-call | tf_op jit(solution)/shard_map/jit(_solve_triangular)/triangular_solve | solution.py:58
  316.6 0.2 fusion.2
  316.8 2.3 fusion
  (3 shorter events, 0.1 us)
Async XLA Ops:
  7.2 41.4 %copy-start = (bf16[256,128]{1,0:T(8,128)(2,1)S(1)}, bf16[256,128]{1,0:T(8,128)(2,1)}, u32[]{:S(2)}) copy-start(bf16[256,128]{1,0:T(8,128)(2,1)} %param.5) | copy-start | bytes 196612
  7.2 284.0 %all-reduce.2.cloned.1.call-start = ((), (), s32[]{:S(2)}) async-start(), calls=%async_computation.1 | async-start | bytes 131072 | tf_op jit(solution)/shard_map/psum | solution.py:33
Sparse Core Ops, SparseCore 0:
  50.7 240.4 all-reduce.1
where the time goes:
time: 326 us
  waiting for transfers between devices  241 us (74%)
  blocking collectives  35.5 us (11%)
  other arithmetic  25.2 us (8%)
  between operations  14.1 us (4%)
  matrix products  5.37 us (2%)
  local copies, waits for them, and re-layouts  5.09 us (2%)
    psum x1, waiting for transfers between devices, global_factor(): gram_matrix = lax.psum(partial_gram, ('slab', 'tile'))  241 us
    all_to_all x1, blocking collectives, local(): lax.all_to_all(outgoing, 'tile', split_axis=0, concat_axis=0, tiled=True)  35.5 us
    another operation x3, other arithmetic, global_factor(): return jnp.linalg.cholesky(gram_matrix)  12.4 us
    another operation x1, other arithmetic, local(): jax.scipy.linalg.solve_triangular(lower_factor, identity, lower=True)  9.81 us
  transfers between devices with their start and end apart: 1, of which 1 were waited for; matrix products, arithmetic and copies ran while one was open for 0% of the time, Pallas kernels for 0%

commit v1 on v0

--- a/solution.py
+++ b/solution.py
@@ -30,7 +30,7 @@
 
 
 def global_factor(partial_gram):
-    gram_matrix = lax.psum(partial_gram, ("slab", "tile"))
+    gram_matrix = lax.psum(lax.psum(partial_gram, "slab"), "tile")
     return jnp.linalg.cholesky(gram_matrix)
 
 

time: 326 us -> 300 us (0.920)
  waiting for transfers between devices: 241 us -> 213 us
    psum x1 -> x2, waiting for transfers between devices: 241 us -> 213 us  [global_factor(): gram_matrix = lax.psum(lax.psum(partial_gram, 'slab'), 'tile')]
  transfers between devices with their start and end apart: 1 -> 2, of which waited for: 1 -> 2; matrix products, arithmetic and copies ran while one was open for 0% -> 0% of each run, Pallas kernels for 0% -> 0%
where the time goes in v1:
time: 300 us; the launch traced here: 299 us
  waiting for transfers between devices  213 us (71%)
  blocking collectives  35.5 us (12%)
  other arithmetic  25.2 us (8%)
  between operations  14.1 us (5%)
  matrix products  5.37 us (2%)
  local copies, waits for them, and re-layouts  5.09 us (2%)
    psum x2, waiting for transfers between devices, global_factor(): gram_matrix = lax.psum(lax.psum(partial_gram, 'slab'), 'tile')  213 us
    all_to_all x1, blocking collectives, local(): lax.all_to_all(outgoing, 'tile', split_axis=0, concat_axis=0, tiled=True)  35.5 us
    another operation x3, other arithmetic, global_factor(): return jnp.linalg.cholesky(gram_matrix)  12.4 us
    another operation x1, other arithmetic, local(): jax.scipy.linalg.solve_triangular(lower_factor, identity, lower=True)  9.81 us
  transfers between devices with their start and end apart: 2, of which 2 were waited for; matrix products, arithmetic and copies ran while one was open for 0% of the time, Pallas kernels for 0%

profile of v1, /device:TPU:1, one launch (start us, length us, event | category | flops | bytes accessed | tf_op | source)
XLA Modules:
  0.0 298.8 jit_solution(3033724374802596473)
XLA Ops:
  7.2 0.0 copy-start
  7.2 0.0 all-reduce.3.cloned.1.call-start
  7.2 0.7 fusion.5
  7.9 0.2 reduce_window_sum.11
  8.1 0.7 fusion.6
  8.8 2.8 copy.17
  11.6 0.8 convolution_convert_fusion
  12.4 0.6 copy.18
  13.0 35.5 %all_to_all.5 = bf16[4,10,128,256]{3,2,1,0:T(8,128)(2,1)S(1)} all-to-all(bf16[4,10,128,256]{3,2,1,0:T(8,128)(2,1)S(1)} %bitcast.35), channel_id=1, replica_groups=mesh['slab'=64,'tile'=4] {'tile'}, dimensions={0} | all-to-all | bytes 5242880 | tf_op jit(solution)/shard_map/all_to_all | solution.py:47
  48.6 0.0 copy-done
  48.6 0.8 convolution_convert_fusion.1
  49.4 1.2 convolution_bitcast_fusion
  50.6 0.0 all-reduce.3.cloned.1.call-update
  50.6 0.0 all-reduce.5.cloned.1.call-start
  50.7 170.3 %all-reduce.3.cloned.1.call-done = f32[128,128]{0,1:T(8,128)} async-done(((f32[128,128]{0,1:T(8,128)}), f32[128,128]{0,1:T(8,128)}) %all-reduce.3.cloned.1.call-update) | async-done | bytes 65552 | tf_op jit(solution)/shard_map/psum | solution.py:33
  221.0 0.0 all-reduce.5.cloned.1.call-update
  221.0 43.1 %all-reduce.5.cloned.1.call-done = f32[128,128]{0,1:T(8,128)} async-done(((f32[128,128]{0,1:T(8,128)}), f32[128,128]{0,1:T(8,128)}) %all-reduce.5.cloned.1.call-update) | async-done | bytes 65552 | tf_op jit(solution)/shard_map/psum | solution.py:33
  264.1 0.9 copy.11
  265.0 0.9 fusion.4
  265.9 11.7 %cholesky.17 = f32[128,128]{1,0:T(8,128)S(1)} custom-call(f32[128,128]{1,0:T(8,128)S(1)} %fusion.4), custom_call_target="Cholesky" | custom-call | tf_op jit(solution)/shard_map/jit(cholesky)/cholesky | solution.py:34
  277.6 0.6 compare_reduce_fusion
  278.3 0.7 multiply_bitcast_fusion
  278.9 0.7 copy.12
  279.7 9.8 %custom-call.7 = f32[1,128,128]{1,2,0:T(8,128)S(1)} custom-call(f32[1,128,128]{2,1,0:T(8,128)S(1)} %get-tuple-element.7), custom_call_target="InvertDiagBlocksLowerTriangular" | custom-call | tf_op jit(solution)/shard_map/jit(_solve_triangular)/triangular_solve | solution.py:58
  289.5 0.2 fusion.2
  289.7 2.3 fusion
  (3 shorter events, 0.1 us)
Async XLA Ops:
  7.2 41.4 %copy-start = (bf16[256,128]{1,0:T(8,128)(2,1)S(1)}, bf16[256,128]{1,0:T(8,128)(2,1)}, u32[]{:S(2)}) copy-start(bf16[256,128]{1,0:T(8,128)(2,1)} %param.5) | copy-start | bytes 196612
  7.2 213.8 %all-reduce.3.cloned.1.call-start = ((), (), s32[]{:S(2)}) async-start(), calls=%async_computation.1 | async-start | bytes 131072 | tf_op jit(solution)/shard_map/psum | solution.py:33
  50.6 213.5 %all-reduce.5.cloned.1.call-start = ((), (), s32[]{:S(2)}) async-start(), calls=%async_computation.2 | async-start | bytes 131072 | tf_op jit(solution)/shard_map/psum | solution.py:33
Sparse Core Ops, SparseCore 0:
  50.7 170.2 all-reduce.2
  223.3 40.7 all-reduce.4
